TPU v7x, 128 devices: a whole 4x4x4 slice. The times are simulated.
128 devices in a mesh: seq: 8 (over z, core), head: 8 (over x_hi, y), batch: 2 (over x_lo).
Axes of the slice: x: 4 (x_hi: 2, x_lo: 2; x = x_hi * 2 + x_lo), y: 4, z: 4, core: 2. Of those that a mesh axis runs over, the one named last changes fastest.
Arguments:
- tokens: bfloat16 [16384, 2048], P(('batch', 'seq')), parts along dimension 0, may hold values from -256 to 256
- w_shared: bfloat16 [2048, 2048], P(None, 'head'), may hold values from -0.125 to 0.125
- w_value: bfloat16 [2048, 2048], P(None, 'head'), may hold values from -0.125 to 0.125
- w_output: bfloat16 [2048, 2048], P('head'), may hold values from -0.125 to 0.125
- doc_length: int32 [2], P('batch'), parts along dimension 0, may hold values from 2048 to 8192
Outputs:
- attended: bfloat16 [16384, 2048], P(('batch', 'seq'), 'head'), parts along dimension 0
There are 2 independent parts, one for each index of `batch`. A program takes and returns all parts, laid end to end along the dimension named above; an argument that names none is the same for every part. Nothing has to cross between parts.
All inputs are finite; a program needn't handle non-finite values.
Results may differ from a plain program's by a relative error of at most 0.018.
Values may be sent and summed in bfloat16 or wider, within the bound.
No kernel may reach another device: no remote copies, remote signals or barrier semaphores. Data moves between devices by JAX's collectives and lax.ppermute only.
A program may use at most 192 MiB of HBM per device.

v0:
```python
import functools
import math

import jax
import jax.numpy as jnp
from jax import lax
from jax.experimental import pallas as pl
from jax.experimental.pallas import tpu as pltpu
from jax.sharding import PartitionSpec as P

HEAD_DIM = 128
LOG2E = 1.4426950408889634
NORM_LIMIT = 60.0
EXTRA = 16
VMEM = 65280 * 2**10
NT = (((1,), (1,)), ((), ()))
ANY = pl.BlockSpec(memory_space=pl.ANY)
HERE = pl.BlockSpec(memory_space=pltpu.VMEM)
SMEM = pl.BlockSpec(memory_space=pltpu.SMEM)
F32 = jnp.float32
BF16 = jnp.bfloat16


def own_core():
    return lax.rem(lax.axis_index("seq"), 2)


def block_start(by, other, rows):
    seq = lax.axis_index("seq")
    place = lax.rem(lax.div(seq, 2) + by, 4) * 2
    core = lax.rem(seq, 2)
    return (place + (1 - core if other else core)) * rows


def start_all(copies):
    for copy in copies:
        copy.start()
    return copies


def project_kernel(x_ref, ws_ref, wv_ref, own_ref, given_ref, x_scr, w_scr, out_scr, sem, out_sem):
    rows, _ = x_ref.shape
    cuts = x_scr.shape[0]
    step = rows // cuts
    wide = 2 * HEAD_DIM
    weights = start_all(
        [
            pltpu.make_async_copy(ws_ref, w_scr.at[:, pl.ds(0, wide)], sem.at[0]),
            pltpu.make_async_copy(wv_ref, w_scr.at[:, pl.ds(wide, wide)], sem.at[1]),
        ]
    )
    tokens = start_all(
        [
            pltpu.make_async_copy(x_ref.at[pl.ds(i * step, step)], x_scr.at[i], sem.at[2 + i])
            for i in range(cuts)
        ]
    )
    core = own_core()
    outs = []

    def send(low, size):
        here = pl.ds(low, size)
        for h, ref in ((core, own_ref), (1 - core, given_ref)):
            outs.extend(
                start_all(
                    [
                        pltpu.make_async_copy(
                            out_scr.at[h, here], ref.at[here], out_sem.at[len(outs)]
                        )
                    ]
                )
            )

    row = lax.broadcasted_iota(jnp.int32, (EXTRA, wide), 0)
    extra = [jnp.zeros((EXTRA, wide), F32) for _ in range(2)]
    largest = [jnp.zeros((8, wide), F32) for _ in range(2)]
    ones = jnp.ones((8, HEAD_DIM), BF16)
    for copy in weights:
        copy.wait()
    for i in range(cuts):
        tokens[i].wait()
        both = jnp.dot(x_scr[i], w_scr[...], preferred_element_type=F32).astype(BF16)
        here = slice(i * step, (i + 1) * step)
        for h in range(2):
            at = h * HEAD_DIM
            out_scr[h, here, :HEAD_DIM] = both[:, at : at + HEAD_DIM]
            out_scr[h, here, HEAD_DIM:] = both[:, wide + at : wide + at + HEAD_DIM]
        send(i * step, step)
        for h in range(2):
            keys = both[:, h * HEAD_DIM : (h + 1) * HEAD_DIM].astype(F32)
            square = keys * keys
            total = lax.dot_general(ones, square.astype(BF16), NT, preferred_element_type=F32)
            largest[h] = jnp.maximum(largest[h], total)
            factor = lax.rsqrt(total / HEAD_DIM + 1e-06) * (LOG2E / math.sqrt(HEAD_DIM))
            first = factor.astype(BF16).astype(F32)
            extra[h] = jnp.where(row == i, jnp.concatenate([first] * 2), extra[h])
            extra[h] = jnp.where(row == 4 + i, jnp.concatenate([factor - first] * 2), extra[h])
    for h in range(2):
        top = jnp.broadcast_to(jnp.max(largest[h]), (EXTRA, wide))
        out_scr[h, rows:, :] = jnp.where(row >= 8, top, extra[h]).astype(BF16)
    send(rows, EXTRA)
    for copy in outs:
        copy.wait()


def project(tokens, w_shared, w_value):
    rows, width = tokens.shape
    cuts = 4
    out = jax.ShapeDtypeStruct((rows + EXTRA, 2 * HEAD_DIM), BF16)
    return pl.pallas_call(
        project_kernel,
        in_specs=[ANY] * 3,
        out_specs=(ANY, ANY),
        out_shape=(out, out),
        scratch_shapes=[
            pltpu.VMEM((cuts, rows // cuts, width), BF16),
            pltpu.VMEM((width, 4 * HEAD_DIM), BF16),
            pltpu.VMEM((2, rows + EXTRA, 2 * HEAD_DIM), BF16),
            pltpu.SemaphoreType.DMA((2 + cuts,)),
            pltpu.SemaphoreType.DMA((2 * cuts + 2,)),
        ],
        compiler_params=pltpu.CompilerParams(vmem_limit_bytes=VMEM),
        cost_estimate=pl.CostEstimate(
            flops=2 * rows * width * 512, bytes_accessed=7 * 2**20, transcendentals=0
        ),
        name="project",
    )(tokens, w_shared, w_value)


def spread_kernel(w_ref, after_ref, out_ref, scr, sem):
    del after_ref
    mine = w_ref.at[pl.ds(pl.multiple_of(own_core() * HEAD_DIM, HEAD_DIM), HEAD_DIM)]
    pltpu.sync_copy(mine, scr)
    for copy in start_all(
        [pltpu.make_async_copy(scr, out_ref.at[i], sem.at[i]) for i in range(4)]
    ):
        copy.wait()


def spread(w_output, after):
    piece = (HEAD_DIM, w_output.shape[1])
    return pl.pallas_call(
        spread_kernel,
        in_specs=[ANY] * 2,
        out_specs=ANY,
        out_shape=jax.ShapeDtypeStruct((4, *piece), BF16),
        scratch_shapes=[pltpu.VMEM(piece, BF16), pltpu.SemaphoreType.DMA((4,))],
        compiler_params=pltpu.CompilerParams(vmem_limit_bytes=VMEM),
        name="spread",
    )(w_output, after)


def attend_kernel(places, first, last, doc_ref, *refs):
    count = len(places)
    if first:
        kv_refs, refs = refs[:count], refs[count:]
        out_ref, kv_scr, acc, sem, acc_sem = refs
        copies = []
    else:
        q_refs, kv_refs, refs = refs[:2], refs[2 : 2 + count], refs[2 + count :]
        if last:
            states, rest, refs = refs[:2], refs[2:6], refs[6:]
            out_ref, kv_scr, acc, sem, acc_sem, q_scr, sums, sums_sem, peak, weight_sum = refs
        else:
            out_ref, kv_scr, acc, sem, acc_sem, q_scr = refs
        copies = start_all(
            [
                pltpu.make_async_copy(q_refs[q], q_scr.at[q], acc_sem.at[2 + q])
                for q in range(2)
            ]
        )
    rows = kv_scr.shape[1] - EXTRA
    tile = 512
    blocks = start_all(
        [pltpu.make_async_copy(kv_refs[i], kv_scr.at[i], sem.at[i]) for i in range(count)]
    )
    if last:
        added = start_all(
            [pltpu.make_async_copy(states[i], sums.at[i], sums_sem.at[i]) for i in range(2)]
        )
    acc[...] = jnp.zeros_like(acc)
    for copy in copies:
        copy.wait()
    doc_len = doc_ref[0]
    q_starts = [block_start(0, other, rows) for other in (False, True)]
    active = jnp.minimum(q_starts[0], q_starts[1]) < doc_len
    starts = [block_start(*place, rows) for place in places]
    q_all = kv_scr if first else q_scr
    for copy in blocks if first else blocks[:1]:
        copy.wait()

    def absorb_block(at, carry):
        q, i = lax.div(at, count), lax.rem(at, count)
        start = starts[0]
        for j in range(1, count):
            start = jnp.where(i == j, starts[j], start)
        if not first:

            @pl.when((q == 0) & (i > 0))
            def _():
                pltpu.make_async_copy(kv_refs[0], kv_scr.at[i], sem.at[i]).wait()

        @pl.when(active & (start < doc_len))
        def _():
            extra = kv_scr[i, rows : rows + 8, :].astype(F32)
            factor = extra[0:4] + extra[4:8]
            queries = q_all[q, :rows, :HEAD_DIM]
            total = acc[q]
            for cut in range(rows // tile):
                keys = slice(cut * tile, (cut + 1) * tile)
                each = tile // 256
                scale = jnp.concatenate(
                    [factor[cut * each + j : cut * each + j + 1] for j in range(each)], axis=1
                )
                place = lax.broadcasted_iota(jnp.int32, (1, tile), 1) + (start + cut * tile)
                bias = jnp.where(place < doc_len, 0.0, -1e30)
                scores = lax.dot_general(
                    queries, kv_scr[i, keys, :HEAD_DIM], NT, preferred_element_type=F32
                )
                weights = jnp.exp2(scores * scale + bias)
                if first:
                    apart = jnp.where(i == q, cut * tile, 4 * rows)
                    weights = jnp.where(
                        lax.broadcasted_iota(jnp.int32, weights.shape, 0)
                        == lax.broadcasted_iota(jnp.int32, weights.shape, 1) + apart,
                        0.0,
                        weights,
                    )
                values = jnp.concatenate(
                    [kv_scr[i, keys, HEAD_DIM:], jnp.ones((tile, HEAD_DIM), BF16)], axis=1
                )
                total += jnp.dot(weights.astype(BF16), values, preferred_element_type=F32)
            acc[q] = total

        return carry

    def leave(q):
        return pltpu.make_async_copy(acc.at[q], out_ref.at[q], acc_sem.at[q])

    lax.fori_loop(0, count, absorb_block, 0)
    if not last:
        leave(0).start()
    lax.fori_loop(count, 2 * count, absorb_block, 0)
    if not last:
        leave(1).start()
        leave(0).wait()
        leave(1).wait()
        return

    for copy in added:
        copy.wait()
    norm = jnp.maximum(
        jnp.max(q_scr[0, rows + 8 :, :].astype(F32)), jnp.max(q_scr[1, rows + 8 :, :].astype(F32))
    )

    @pl.when(norm > NORM_LIMIT**2)
    def _():
        peak[...] = jnp.full_like(peak, -1e30)
        weight_sum[...] = jnp.zeros_like(weight_sum)
        acc[...] = jnp.zeros_like(acc)
        sums[...] = jnp.zeros_like(sums)
        near = ((3, False), (3, True), (1, False), (1, True))
        everything = [
            (q_refs[0], (0, False)),
            (q_refs[1], (0, True)),
            *zip(rest, near),
            *zip(kv_refs, places),
        ]
        small = 256
        for block_ref, place in everything:
            pltpu.sync_copy(block_ref, kv_scr.at[0])
            key_start = block_start(*place, rows)
            extra = kv_scr[0, rows : rows + 8, :].astype(F32)
            factor = extra[0:4] + extra[4:8]

            def absorb(at, carry, key_start=key_start, factor=factor):
                q = lax.div(at, rows // small)
                low = pl.multiple_of(lax.rem(at, rows // small) * small, small)
                here = pl.ds(low, small)
                query_start = jnp.where(q == 0, q_starts[0], q_starts[1]) + low
                for cut in range(rows // small):
                    keys = slice(cut * small, (cut + 1) * small)
                    scores = lax.dot_general(
                        q_scr[q, here, :HEAD_DIM], kv_scr[0, keys, :HEAD_DIM], NT, preferred_element_type=F32
                    )
                    key_pos = lax.broadcasted_iota(jnp.int32, scores.shape, 1) + (
                        key_start + cut * small
                    )
                    query_pos = lax.broadcasted_iota(jnp.int32, scores.shape, 0) + query_start
                    allowed = (key_pos < doc_len) & (key_pos != query_pos)
                    scores = jnp.where(allowed, scores * factor[cut : cut + 1], -1e30)
                    old = peak[q, here, :]
                    new = jnp.maximum(old, jnp.max(scores, axis=1, keepdims=True))
                    weights = jnp.where(allowed, jnp.exp2(scores - new[:, :1]), 0.0)
                    rescale = jnp.exp2(old - new)
                    peak[q, here, :] = new
                    weight_sum[q, here, :] = weight_sum[q, here, :] * rescale + jnp.sum(
                        weights, axis=1, keepdims=True
                    )
                    acc[q, here, :HEAD_DIM] = acc[q, here, :HEAD_DIM] * rescale + jnp.dot(
                        weights.astype(BF16), kv_scr[0, keys, HEAD_DIM:], preferred_element_type=F32
                    )
                return carry

            lax.fori_loop(0, 2 * rows // small, absorb, 0)
        for q in range(2):
            acc[q, :, HEAD_DIM:] = weight_sum[q]

    core = own_core()
    for q in range(2):
        total = acc[q] + (sums[0, q] + sums[1, q])
        inside = lax.broadcasted_iota(jnp.int32, (rows, HEAD_DIM), 0) + q_starts[q] < doc_len
        mixed = jnp.where(inside, total[:, :HEAD_DIM] / total[:, HEAD_DIM:], 0.0)
        block = core if q == 0 else 1 - core
        out_ref[:, block] = mixed.astype(BF16).reshape(4, rows // 4, HEAD_DIM)


def attend(doc_length, queries, blocks, places, states, rest, name):
    rows = blocks[0].shape[0] - EXTRA
    count = len(blocks)
    first, last = queries is None, rest is not None
    out_shape = jax.ShapeDtypeStruct((2, rows, 2 * HEAD_DIM), F32)
    scratch = [
        pltpu.VMEM((count, rows + EXTRA, 2 * HEAD_DIM), BF16),
        pltpu.VMEM(out_shape.shape, F32),
        pltpu.SemaphoreType.DMA((count,)),
        pltpu.SemaphoreType.DMA((4,)),
    ]
    args = list(blocks)
    if not first:
        args = [*queries, *blocks]
        scratch.append(pltpu.VMEM((2, rows + EXTRA, 2 * HEAD_DIM), BF16))
    if last:
        args += [*states, *rest]
        scratch += [
            pltpu.VMEM((2, *out_shape.shape), F32),
            pltpu.SemaphoreType.DMA((2,)),
        ]
        out_shape = jax.ShapeDtypeStruct((4, 2, rows // 4, HEAD_DIM), BF16)
        scratch += [
            pltpu.VMEM((2, rows, HEAD_DIM), F32),
            pltpu.VMEM((2, rows, HEAD_DIM), F32),
        ]
    return pl.pallas_call(
        functools.partial(attend_kernel, places, first, last),
        in_specs=[SMEM] + [ANY] * len(args),
        out_specs=HERE if last else ANY,
        out_shape=out_shape,
        scratch_shapes=scratch,
        compiler_params=pltpu.CompilerParams(vmem_limit_bytes=VMEM),
        cost_estimate=pl.CostEstimate(
            flops=16 * rows * rows * count * HEAD_DIM,
            bytes_accessed=4 * 2**20,
            transcendentals=0,
        ),
        name=name,
    )(doc_length, *args)


def output_kernel(ctx_ref, got_ref, w_ref, w_got_ref, out_ref):
    core = own_core()
    lefts = [
        jnp.concatenate([ref[y, core] for y in range(4)], axis=1) for ref in (ctx_ref, got_ref)
    ]
    width = w_ref.shape[2]
    step = width // 8
    for i in range(8):
        cols = slice(i * step, (i + 1) * step)
        part = None
        for left, ref in zip(lefts, (w_ref, w_got_ref)):
            right = ref[:, :, cols].reshape(4 * HEAD_DIM, step)
            term = jnp.dot(left, right, preferred_element_type=F32)
            part = term if part is None else part + term
        out_ref[i] = part.astype(BF16)


def output(context, got, weights, weights_got):
    rows = context.shape[2]
    width = weights.shape[2]
    return pl.pallas_call(
        output_kernel,
        in_specs=[HERE] * 4,
        out_specs=HERE,
        out_shape=jax.ShapeDtypeStruct((8, rows, width // 8), BF16),
        compiler_params=pltpu.CompilerParams(vmem_limit_bytes=30 * 2**20),
        cost_estimate=pl.CostEstimate(
            flops=2 * rows * width * 1024, bytes_accessed=6 * 2**20, transcendentals=0
        ),
        name="output",
    )(context, got, weights, weights_got)


def body(tokens, w_shared, w_value, w_output, doc_length):
    def move(array, by, cross):
        return lax.ppermute(
            array, "seq", [(i, (i // 2 + by) % 4 * 2 + (i % 2 ^ cross)) for i in range(8)]
        )

    own, given = project(tokens, w_shared, w_value)
    peer = move(given, 0, 1)
    own_left, peer_right = move(own, 1, 0), move(given, -1, 1)
    peer_left, own_right = move(given, 1, 1), move(own, -1, 0)

    queries = (own, peer)
    here = attend(doc_length, None, queries, ((0, False), (0, True)), None, None, "attend_here")
    y_groups = [[0, 1, 2, 3], [4, 5, 6, 7]]
    weights = lax.all_to_all(
        spread(w_output, here), "head", 0, 0, axis_index_groups=y_groups, tiled=True
    )
    own_left, peer_right, here = lax.optimization_barrier((own_left, peer_right, here))
    own_far, peer_far = move(own_left, 1, 0), move(peer_right, -1, 0)
    blocks = (own_left, peer_left, own_right, peer_right)
    near = attend(
        doc_length,
        queries,
        blocks,
        ((3, False), (3, True), (1, False), (1, True)),
        None,
        None,
        "attend_near",
    )
    context = attend(
        doc_length,
        queries,
        (own_far, peer_far),
        ((2, False), (2, True)),
        (here, near),
        blocks,
        "attend_far",
    )
    weights, context = lax.optimization_barrier((weights, context))
    weights_got = move(weights, 0, 1)
    context = lax.all_to_all(context, "head", 0, 0, axis_index_groups=y_groups, tiled=True)
    terms = output(context, move(context, 0, 1), weights, weights_got)
    terms = lax.all_to_all(terms, "head", 0, 0, tiled=True).astype(F32)
    result = (terms[:4] + terms[4:]).astype(BF16)
    return result.reshape(tokens.shape[0], result.shape[-1])


def solution(mesh):
    placed = (
        P(("batch", "seq"), None),
        P(None, "head"),
        P(None, "head"),
        P("head", None),
        P("batch"),
    )
    return jax.shard_map(
        body, mesh=mesh, in_specs=placed, out_specs=P(("batch", "seq"), "head"), check_vma=False
    )
```

profile of v0, /device:TPU:0, one launch (start us, length us, event | category | flops | bytes accessed | tf_op | source)
XLA Modules:
  0.0 193.7 jit_solution(17512363172064151015)
XLA Ops:
  0.0 6.1 %project.1 = (bf16[1040,256]{1,0:T(8,128)(2,1)}, bf16[1040,256]{1,0:T(8,128)(2,1)}) custom-call(bf16[1024,2048]{1,0:T(8,128)(2,1)} %x_ref.1, bf16[2048,256]{1,0:T(8,128)(2,1)} %ws_ref.1, bf16[2048,256]{1,0:T(8,128)(2,1)} %wv_ref.1), custom_call_target="tpu_custom_call" | custom-call | flops 2147483648 | bytes 7340032 | tf_op jit(solution)/shard_map/project/pallas_call | solution.py:110
  6.1 0.1 collective-permute-start
  6.2 2.1 %collective-permute-start.5 = (bf16[1040,256]{1,0:T(8,128)(2,1)}, bf16[1040,256]{1,0:T(8,128)(2,1)}, u32[]{:S(2)}, u32[]{:S(2)}) collective-permute-start(bf16[1040,256]{1,0:T(8,128)(2,1)} %get-tuple-element.13), channel_id=1, source_target_pairs={{0,48},{16,32},{32,80},{48,64},{64,112},{80,96},{96,16},{112,0},{1... | collective-permute-start | bytes 1597448 | tf_op jit(solution)/shard_map/ppermute | solution.py:395
  8.3 2.1 %collective-permute-start.2 = (bf16[1040,256]{1,0:T(8,128)(2,1)}, bf16[1040,256]{1,0:T(8,128)(2,1)}, u32[]{:S(2)}, u32[]{:S(2)}) collective-permute-start(bf16[1040,256]{1,0:T(8,128)(2,1)} %get-tuple-element.13), channel_id=1, source_target_pairs={{0,112},{16,96},{32,16},{48,0},{64,48},{80,32},{96,80},{112,64},{1... | collective-permute-start | bytes 1597448 | tf_op jit(solution)/shard_map/ppermute | solution.py:395
  10.4 1.7 collective-permute-start.6
  12.1 0.3 collective-permute-start.1
  13.1 0.0 collective-permute-done.refs_1_
  13.1 7.7 %attend_here.1.after_ref.refs_4_ = f32[2,1024,256]{2,1,0:T(8,128)} custom-call(s32[1]{0:T(128)S(6)} %copy.6.doc_ref, bf16[1040,256]{1,0:T(8,128)(2,1)} %get-tuple-element.12.refs_0_, bf16[1040,256]{1,0:T(8,128)(2,1)} %collective-permute-done.refs_1_), custom_call_target="tpu_custom_call" | custom-call | flops 4294967296 | bytes 4194304 | tf_op jit(solution)/shard_map/attend_here/pallas_call | solution.py:344
  20.8 2.4 %spread.1 = bf16[4,128,2048]{2,1,0:T(8,128)(2,1)} custom-call(bf16[256,2048]{1,0:T(8,128)(2,1)} %w_ref.1, f32[2,1024,256]{2,1,0:T(8,128)} %attend_here.1.after_ref.refs_4_), custom_call_target="tpu_custom_call" | custom-call | tf_op jit(solution)/shard_map/spread/pallas_call | solution.py:142
  23.3 4.5 %all-to-all-start = ((bf16[4,128,2048]{2,1,0:T(8,128)(2,1)}), bf16[4,128,2048]{2,1,0:T(8,128)(2,1)}, u32[]{:S(2)}, u32[]{:S(2)}) async-start(bf16[4,128,2048]{2,1,0:T(8,128)(2,1)} %spread.1), calls=%async_computation | async-start | bytes 4194304 | tf_op jit(solution)/shard_map/all_to_all | solution.py:407
  27.7 0.0 collective-permute-done.2.refs_5_.refs_9_
  27.7 7.0 %collective-permute-done.1.refs_2_.refs_6_ = bf16[1040,256]{1,0:T(8,128)(2,1)} collective-permute-done((bf16[1040,256]{1,0:T(8,128)(2,1)}, bf16[1040,256]{1,0:T(8,128)(2,1)}, u32[]{:S(2)}, u32[]{:S(2)}) %collective-permute-start.1) | collective-permute-done | bytes 532512 | tf_op jit(solution)/shard_map/ppermute | solution.py:395
  34.8 0.0 collective-permute-start.3
  34.8 3.2 %collective-permute-start.4 = (bf16[1040,256]{1,0:T(8,128)(2,1)}, bf16[1040,256]{1,0:T(8,128)(2,1)}, u32[]{:S(2)}, u32[]{:S(2)}) collective-permute-start(bf16[1040,256]{1,0:T(8,128)(2,1)} %collective-permute-done.2.refs_5_.refs_9_), channel_id=1, source_target_pairs={{0,96},{16,112},{32,0},{48,16},{64,32},{80,48},{96,64},{112,80},{1... | collective-permute-start | bytes 1597448 | tf_op jit(solution)/shard_map/ppermute | solution.py:395
  38.0 0.0 collective-permute-done.5.refs_3_.refs_7_
  38.0 0.0 collective-permute-done.6.refs_4_.refs_8_
  38.0 8.3 %attend_near.1.refs_5_ = f32[2,1024,256]{2,1,0:T(8,128)} custom-call(s32[1]{0:T(128)S(6)} %copy.6.doc_ref, bf16[1040,256]{1,0:T(8,128)(2,1)} %get-tuple-element.12.refs_0_, bf16[1040,256]{1,0:T(8,128)(2,1)} %collective-permute-done.refs_1_, bf16[1040,256]{1,0:T(8,128)(2,1)} %collective-permute-done.1.refs_2_.refs_6_, ...), custom_call_target="tpu_custom_call" | custom-call | flops 8589934592 | bytes 4194304 | tf_op jit(solution)/shard_map/attend_near/pallas_call | solution.py:344
  46.4 3.8 %collective-permute-done.3.refs_2_ = bf16[1040,256]{1,0:T(8,128)(2,1)} collective-permute-done((bf16[1040,256]{1,0:T(8,128)(2,1)}, bf16[1040,256]{1,0:T(8,128)(2,1)}, u32[]{:S(2)}, u32[]{:S(2)}) %collective-permute-start.3) | collective-permute-done | bytes 532512 | tf_op jit(solution)/shard_map/ppermute | solution.py:395
  50.2 0.0 collective-permute-done.4.refs_3_
  50.2 100.8 %attend_far.1 = bf16[4,2,256,128]{3,2,1,0:T(8,128)(2,1)} custom-call(s32[1]{0:T(128)S(6)} %copy.6.doc_ref, bf16[1040,256]{1,0:T(8,128)(2,1)} %get-tuple-element.12.refs_0_, bf16[1040,256]{1,0:T(8,128)(2,1)} %collective-permute-done.refs_1_, bf16[1040,256]{1,0:T(8,128)(2,1)} %collective-permute-done.3.refs_2_, ...), custom_call_target="tpu_custom_call" | custom-call | flops 4294967296 | bytes 4194304 | tf_op jit(solution)/shard_map/attend_far/pallas_call | solution.py:344
  151.0 0.0 all-to-all-done.w_ref
  151.0 0.1 collective-permute-start.8
  151.1 14.6 %all_to_all.15.ctx_ref = bf16[4,2,256,128]{3,2,1,0:T(8,128)(2,1)S(1)} all-to-all(bf16[4,2,256,128]{3,2,1,0:T(8,128)(2,1)} %attend_far.1), channel_id=1, replica_groups={{0,2,4,6},{8,10,12,14},{1,3,5,7},{9,11,13,15},{16,18,20,22},{24,26,28,3..., dimensions={0} | all-to-all | bytes 1048576 | tf_op jit(solution)/shard_map/all_to_all | solution.py:433
  165.7 0.0 collective-permute-start.7
  165.7 1.9 collective-permute-done.7.got_ref
  167.6 0.0 collective-permute-done.8.w_got_ref
  167.6 2.8 %output.1 = bf16[8,256,256]{2,1,0:T(8,128)(2,1)S(1)} custom-call(bf16[4,2,256,128]{3,2,1,0:T(8,128)(2,1)S(1)} %all_to_all.15.ctx_ref, bf16[4,2,256,128]{3,2,1,0:T(8,128)(2,1)S(1)} %collective-permute-done.7.got_ref, bf16[4,128,2048]{2,1,0:T(8,128)(2,1)} %all-to-all-done.w_ref, bf16[4,128,2048]{2,1,0:T(8,128)(2,1)S(1)} %collective-permute-done.8.w_got_ref), custom_call_target="tpu_custom_call" | custom-call | flops 1073741824 | bytes 6291456 | tf_op jit(solution)/shard_map/output/pallas_call | solution.py:380
  170.4 22.2 %all_to_all.16 = bf16[8,256,256]{2,1,0:T(8,128)(2,1)S(1)} all-to-all(bf16[8,256,256]{2,1,0:T(8,128)(2,1)S(1)} %output.1), channel_id=1, replica_groups=mesh['seq'=8,'head'=8,'batch'=2] {'head'}, dimensions={0} | all-to-all | bytes 2097152 | tf_op jit(solution)/shard_map/all_to_all | solution.py:435
  192.6 0.2 convert_element_type.6
  192.8 0.9 fusion
Async XLA Ops:
  6.1 7.0 %collective-permute-start = (bf16[1040,256]{1,0:T(8,128)(2,1)}, bf16[1040,256]{1,0:T(8,128)(2,1)}, u32[]{:S(2)}, u32[]{:S(2)}) collective-permute-start(bf16[1040,256]{1,0:T(8,128)(2,1)} %get-tuple-element.13), channel_id=1, source_target_pairs={{0,16},{16,0},{32,48},{48,32},{64,80},{80,64},{96,112},{112,96},{1... | collective-permute-start | bytes 1597448 | tf_op jit(solution)/shard_map/ppermute | solution.py:395
  6.2 31.8 %collective-permute-start.5 = (bf16[1040,256]{1,0:T(8,128)(2,1)}, bf16[1040,256]{1,0:T(8,128)(2,1)}, u32[]{:S(2)}, u32[]{:S(2)}) collective-permute-start(bf16[1040,256]{1,0:T(8,128)(2,1)} %get-tuple-element.13), channel_id=1, source_target_pairs={{0,48},{16,32},{32,80},{48,64},{64,112},{80,96},{96,16},{112,0},{1... | collective-permute-start | bytes 1597448 | tf_op jit(solution)/shard_map/ppermute | solution.py:395
  8.3 19.4 %collective-permute-start.2 = (bf16[1040,256]{1,0:T(8,128)(2,1)}, bf16[1040,256]{1,0:T(8,128)(2,1)}, u32[]{:S(2)}, u32[]{:S(2)}) collective-permute-start(bf16[1040,256]{1,0:T(8,128)(2,1)} %get-tuple-element.13), channel_id=1, source_target_pairs={{0,112},{16,96},{32,16},{48,0},{64,48},{80,32},{96,80},{112,64},{1... | collective-permute-start | bytes 1597448 | tf_op jit(solution)/shard_map/ppermute | solution.py:395
  10.4 27.6 %collective-permute-start.6 = (bf16[1040,256]{1,0:T(8,128)(2,1)}, bf16[1040,256]{1,0:T(8,128)(2,1)}, u32[]{:S(2)}, u32[]{:S(2)}) collective-permute-start(bf16[1040,256]{1,0:T(8,128)(2,1)} %get-tuple-element.12.refs_0_), channel_id=1, source_target_pairs={{0,96},{16,112},{32,0},{48,16},{64,32},{80,48},{96,64},{112,80},{1... | collective-permute-start | bytes 1597448 | tf_op jit(solution)/shard_map/ppermute | solution.py:395
  12.1 22.7 %collective-permute-start.1 = (bf16[1040,256]{1,0:T(8,128)(2,1)}, bf16[1040,256]{1,0:T(8,128)(2,1)}, u32[]{:S(2)}, u32[]{:S(2)}) collective-permute-start(bf16[1040,256]{1,0:T(8,128)(2,1)} %get-tuple-element.12.refs_0_), channel_id=1, source_target_pairs={{0,32},{16,48},{32,64},{48,80},{64,96},{80,112},{96,0},{112,16},{1... | collective-permute-start | bytes 1597448 | tf_op jit(solution)/shard_map/ppermute | solution.py:395
  23.3 127.7 %all-to-all-start = ((bf16[4,128,2048]{2,1,0:T(8,128)(2,1)}), bf16[4,128,2048]{2,1,0:T(8,128)(2,1)}, u32[]{:S(2)}, u32[]{:S(2)}) async-start(bf16[4,128,2048]{2,1,0:T(8,128)(2,1)} %spread.1), calls=%async_computation | async-start | bytes 4194304 | tf_op jit(solution)/shard_map/all_to_all | solution.py:407
  34.8 15.4 %collective-permute-start.3 = (bf16[1040,256]{1,0:T(8,128)(2,1)}, bf16[1040,256]{1,0:T(8,128)(2,1)}, u32[]{:S(2)}, u32[]{:S(2)}) collective-permute-start(bf16[1040,256]{1,0:T(8,128)(2,1)} %collective-permute-done.1.refs_2_.refs_6_), channel_id=1, source_target_pairs={{0,32},{16,48},{32,64},{48,80},{64,96},{80,112},{96,0},{112,16},{1... | collective-permute-start | bytes 1597448 | tf_op jit(solution)/shard_map/ppermute | solution.py:395
  34.8 15.4 %collective-permute-start.4 = (bf16[1040,256]{1,0:T(8,128)(2,1)}, bf16[1040,256]{1,0:T(8,128)(2,1)}, u32[]{:S(2)}, u32[]{:S(2)}) collective-permute-start(bf16[1040,256]{1,0:T(8,128)(2,1)} %collective-permute-done.2.refs_5_.refs_9_), channel_id=1, source_target_pairs={{0,96},{16,112},{32,0},{48,16},{64,32},{80,48},{96,64},{112,80},{1... | collective-permute-start | bytes 1597448 | tf_op jit(solution)/shard_map/ppermute | solution.py:395
  151.0 16.6 %collective-permute-start.8 = (bf16[4,128,2048]{2,1,0:T(8,128)(2,1)}, bf16[4,128,2048]{2,1,0:T(8,128)(2,1)S(1)}, u32[]{:S(2)}, u32[]{:S(2)}) collective-permute-start(bf16[4,128,2048]{2,1,0:T(8,128)(2,1)} %all-to-all-done.w_ref), channel_id=1, source_target_pairs={{0,16},{16,0},{32,48},{48,32},{64,80},{80,64},{96,112},{112,96},{1... | collective-permute-start | bytes 6291464 | tf_op jit(solution)/shard_map/ppermute | solution.py:395
  165.7 1.9 collective-permute-start.7
where the time goes:
time: 195 us; the launch traced here: 194 us
  Pallas kernels  128 us (66%)
  blocking collectives  36.7 us (19%)
  starting transfers between devices  14.1 us (7%)
  waiting for transfers between devices  12.8 us (7%)
    pallas_call x3, Pallas kernels, attend(): pl.pallas_call(functools.partial(attend_kernel, places, first, last), in_...  117 us
    all_to_all x1, blocking collectives, body(): terms = lax.all_to_all(terms, 'head', 0, 0, tiled=True).astype(F32)  22.2 us
    all_to_all x1, blocking collectives, body(): lax.all_to_all(context, 'head', 0, 0, axis_index_groups=y_groups, tiled=T...  14.6 us
    ppermute x9, waiting for transfers between devices, move(): lax.ppermute(array, 'seq', [(i, (i // 2 + by) % 4 * 2 + (i % 2 ^ cross))...  12.8 us
    ppermute x9, starting transfers between devices, move(): lax.ppermute(array, 'seq', [(i, (i // 2 + by) % 4 * 2 + (i % 2 ^ cross))...  9.66 us
    pallas_call x1, Pallas kernels, project(): pl.pallas_call(project_kernel, in_specs=[ANY] * 3, out_specs=(ANY, ANY),...  6.07 us
    all_to_all x1, starting transfers between devices, body(): lax.all_to_all(spread(w_output, here), 'head', 0, 0, axis_index_groups=y_...  4.48 us
  transfers between devices with their start and end apart: 10, of which 3 were waited for; matrix products, arithmetic and copies ran while one was open for 0% of the time, Pallas kernels for 62%

commit v1 on v0

--- a/solution.py
+++ b/solution.py
@@ -189,14 +189,13 @@
     for copy in blocks if first else blocks[:1]:
         copy.wait()
 
-    def absorb_block(at, carry):
-        q, i = lax.div(at, count), lax.rem(at, count)
+    def absorb_block(i, carry):
         start = starts[0]
         for j in range(1, count):
             start = jnp.where(i == j, starts[j], start)
         if not first:
 
-            @pl.when((q == 0) & (i > 0))
+            @pl.when(i > 0)
             def _():
                 pltpu.make_async_copy(kv_refs[0], kv_scr.at[i], sem.at[i]).wait()
 
@@ -204,47 +203,44 @@
         def _():
             extra = kv_scr[i, rows : rows + 8, :].astype(F32)
             factor = extra[0:4] + extra[4:8]
-            queries = q_all[q, :rows, :HEAD_DIM]
-            total = acc[q]
-            for cut in range(rows // tile):
-                keys = slice(cut * tile, (cut + 1) * tile)
-                each = tile // 256
-                scale = jnp.concatenate(
-                    [factor[cut * each + j : cut * each + j + 1] for j in range(each)], axis=1
-                )
-                place = lax.broadcasted_iota(jnp.int32, (1, tile), 1) + (start + cut * tile)
-                bias = jnp.where(place < doc_len, 0.0, -1e30)
-                scores = lax.dot_general(
-                    queries, kv_scr[i, keys, :HEAD_DIM], NT, preferred_element_type=F32
-                )
-                weights = jnp.exp2(scores * scale + bias)
-                if first:
-                    apart = jnp.where(i == q, cut * tile, 4 * rows)
-                    weights = jnp.where(
-                        lax.broadcasted_iota(jnp.int32, weights.shape, 0)
-                        == lax.broadcasted_iota(jnp.int32, weights.shape, 1) + apart,
-                        0.0,
-                        weights,
-                    )
-                values = jnp.concatenate(
-                    [kv_scr[i, keys, HEAD_DIM:], jnp.ones((tile, HEAD_DIM), BF16)], axis=1
-                )
-                total += jnp.dot(weights.astype(BF16), values, preferred_element_type=F32)
-            acc[q] = total
+            for q in range(2):
+                queries = q_all[q, :rows, :HEAD_DIM]
+                total = acc[q]
+                for cut in range(rows // tile):
+                    keys = slice(cut * tile, (cut + 1) * tile)
+                    each = tile // 256
+                    scale = jnp.concatenate(
+                        [factor[cut * each + j : cut * each + j + 1] for j in range(each)], axis=1
+                    )
+                    place = lax.broadcasted_iota(jnp.int32, (1, tile), 1) + (start + cut * tile)
+                    bias = jnp.where(place < doc_len, 0.0, -1e30)
+                    scores = lax.dot_general(
+                        queries, kv_scr[i, keys, :HEAD_DIM], NT, preferred_element_type=F32
+                    )
+                    weights = jnp.exp2(scores * scale + bias)
+                    if first:
+                        apart = jnp.where(i == q, cut * tile, 4 * rows)
+                        weights = jnp.where(
+                            lax.broadcasted_iota(jnp.int32, weights.shape, 0)
+                            == lax.broadcasted_iota(jnp.int32, weights.shape, 1) + apart,
+                            0.0,
+                            weights,
+                        )
+                    values = jnp.concatenate(
+                        [kv_scr[i, keys, HEAD_DIM:], jnp.ones((tile, HEAD_DIM), BF16)], axis=1
+                    )
+                    total += jnp.dot(weights.astype(BF16), values, preferred_element_type=F32)
+                acc[q] = total
 
         return carry
-
-    def leave(q):
-        return pltpu.make_async_copy(acc.at[q], out_ref.at[q], acc_sem.at[q])
 
     lax.fori_loop(0, count, absorb_block, 0)
     if not last:
-        leave(0).start()
-    lax.fori_loop(count, 2 * count, absorb_block, 0)
-    if not last:
-        leave(1).start()
-        leave(0).wait()
-        leave(1).wait()
+        outs = start_all(
+            [pltpu.make_async_copy(acc.at[q], out_ref.at[q], acc_sem.at[q]) for q in range(2)]
+        )
+        for copy in outs:
+            copy.wait()
         return
 
     for copy in added:
@@ -401,11 +397,13 @@
     own_left, peer_right = move(own, 1, 0), move(given, -1, 1)
     peer_left, own_right = move(given, 1, 1), move(own, -1, 0)
 
+    repeated = spread(w_output, peer)
+    peer, repeated = lax.optimization_barrier((peer, repeated))
     queries = (own, peer)
     here = attend(doc_length, None, queries, ((0, False), (0, True)), None, None, "attend_here")
     y_groups = [[0, 1, 2, 3], [4, 5, 6, 7]]
     weights = lax.all_to_all(
-        spread(w_output, here), "head", 0, 0, axis_index_groups=y_groups, tiled=True
+        repeated, "head", 0, 0, axis_index_groups=y_groups, tiled=True
     )
     own_left, peer_right, here = lax.optimization_barrier((own_left, peer_right, here))
     own_far, peer_far = move(own_left, 1, 0), move(peer_right, -1, 0)

time: 195 us -> 192 us (0.985); the launches traced: 194 us -> 194 us
  waiting for transfers between devices: 12.8 us -> 6.41 us
  Pallas kernels: 128 us -> 132 us
  starting transfers between devices: 14.1 us -> 17.3 us
    ppermute x9, waiting for transfers between devices: 12.8 us -> 6.4 us  [move(): lax.ppermute(array, 'seq', [(i, (i // 2 + by) % 4 * 2 + (i % 2 ^ cross))...]
    pallas_call x3, Pallas kernels: 117 us -> 121 us  [attend(): pl.pallas_call(functools.partial(attend_kernel, places, first, last), in_...]
    ppermute x9, starting transfers between devices: 9.66 us -> 12.8 us  [move(): lax.ppermute(array, 'seq', [(i, (i // 2 + by) % 4 * 2 + (i % 2 ^ cross))...]
  transfers between devices with their start and end apart: 10 -> 10, of which waited for: 3 -> 2; matrix products, arithmetic and copies ran while one was open for 0% -> 0% of each run, Pallas kernels for 62% -> 64%
where the time goes in v1:
time: 192 us; the launch traced here: 194 us
  Pallas kernels  132 us (69%)
  blocking collectives  36.1 us (19%)
  starting transfers between devices  17.3 us (9%)
  waiting for transfers between devices  6.41 us (3%)
    pallas_call x3, Pallas kernels, attend(): pl.pallas_call(functools.partial(attend_kernel, places, first, last), in_...  121 us
    all_to_all x1, blocking collectives, body(): terms = lax.all_to_all(terms, 'head', 0, 0, tiled=True).astype(F32)  22.2 us
    all_to_all x1, blocking collectives, body(): lax.all_to_all(context, 'head', 0, 0, axis_index_groups=y_groups, tiled=T...  14 us
    ppermute x9, starting transfers between devices, move(): lax.ppermute(array, 'seq', [(i, (i // 2 + by) % 4 * 2 + (i % 2 ^ cross))...  12.8 us
    ppermute x9, waiting for transfers between devices, move(): lax.ppermute(array, 'seq', [(i, (i // 2 + by) % 4 * 2 + (i % 2 ^ cross))...  6.4 us
    pallas_call x1, Pallas kernels, project(): pl.pallas_call(project_kernel, in_specs=[ANY] * 3, out_specs=(ANY, ANY),...  6.07 us
    all_to_all x1, starting transfers between devices, body(): lax.all_to_all(repeated, 'head', 0, 0, axis_index_groups=y_groups, tiled=...  4.48 us
  transfers between devices with their start and end apart: 10, of which 2 were waited for; matrix products, arithmetic and copies ran while one was open for 0% of the time, Pallas kernels for 64%

profile of v1, /device:TPU:0, one launch (start us, length us, event | category | flops | bytes accessed | tf_op | source)
XLA Modules:
  0.0 193.8 jit_solution(9569166700574290802)
XLA Ops:
  0.0 6.1 %project.1 = (bf16[1040,256]{1,0:T(8,128)(2,1)}, bf16[1040,256]{1,0:T(8,128)(2,1)}) custom-call(bf16[1024,2048]{1,0:T(8,128)(2,1)} %x_ref.1, bf16[2048,256]{1,0:T(8,128)(2,1)} %ws_ref.1, bf16[2048,256]{1,0:T(8,128)(2,1)} %wv_ref.1), custom_call_target="tpu_custom_call" | custom-call | flops 2147483648 | bytes 7340032 | tf_op jit(solution)/shard_map/project/pallas_call | solution.py:110
  6.1 0.1 collective-permute-start
  6.2 4.2 %collective-permute-start.2 = (bf16[1040,256]{1,0:T(8,128)(2,1)}, bf16[1040,256]{1,0:T(8,128)(2,1)}, u32[]{:S(2)}, u32[]{:S(2)}) collective-permute-start(bf16[1040,256]{1,0:T(8,128)(2,1)} %get-tuple-element.14), channel_id=1, source_target_pairs={{0,112},{16,96},{32,16},{48,0},{64,48},{80,32},{96,80},{112,64},{1... | collective-permute-start | bytes 1597448 | tf_op jit(solution)/shard_map/ppermute | solution.py:391
  10.4 0.0 collective-permute-start.1
  10.4 0.0 collective-permute-start.5
  10.4 3.2 %collective-permute-start.6 = (bf16[1040,256]{1,0:T(8,128)(2,1)}, bf16[1040,256]{1,0:T(8,128)(2,1)}, u32[]{:S(2)}, u32[]{:S(2)}) collective-permute-start(bf16[1040,256]{1,0:T(8,128)(2,1)} %get-tuple-element.16.refs_0_), channel_id=1, source_target_pairs={{0,96},{16,112},{32,0},{48,16},{64,32},{80,48},{96,64},{112,80},{1... | collective-permute-start | bytes 1597448 | tf_op jit(solution)/shard_map/ppermute | solution.py:391
  14.3 0.0 collective-permute-done.after_ref.refs_1_
  14.3 2.4 %spread.1 = bf16[4,128,2048]{2,1,0:T(8,128)(2,1)} custom-call(bf16[256,2048]{1,0:T(8,128)(2,1)} %w_ref.1, bf16[1040,256]{1,0:T(8,128)(2,1)} %collective-permute-done.after_ref.refs_1_), custom_call_target="tpu_custom_call" | custom-call | tf_op jit(solution)/shard_map/spread/pallas_call | solution.py:142
  16.7 4.5 %all-to-all-start = ((bf16[4,128,2048]{2,1,0:T(8,128)(2,1)}), bf16[4,128,2048]{2,1,0:T(8,128)(2,1)}, u32[]{:S(2)}, u32[]{:S(2)}) async-start(bf16[4,128,2048]{2,1,0:T(8,128)(2,1)} %spread.1), calls=%async_computation | async-start | bytes 4194304 | tf_op jit(solution)/shard_map/all_to_all | solution.py:405
  21.2 7.5 %attend_here.1.refs_4_ = f32[2,1024,256]{2,1,0:T(8,128)} custom-call(s32[1]{0:T(128)S(6)} %copy.6.doc_ref, bf16[1040,256]{1,0:T(8,128)(2,1)} %get-tuple-element.16.refs_0_, bf16[1040,256]{1,0:T(8,128)(2,1)} %collective-permute-done.after_ref.refs_1_), custom_call_target="tpu_custom_call" | custom-call | flops 4294967296 | bytes 4194304 | tf_op jit(solution)/shard_map/attend_here/pallas_call | solution.py:340
  28.7 0.0 collective-permute-done.2.refs_5_.refs_9_
  28.7 0.0 collective-permute-done.1.refs_2_.refs_6_
  28.7 0.1 collective-permute-start.3
  28.8 3.2 %collective-permute-start.4 = (bf16[1040,256]{1,0:T(8,128)(2,1)}, bf16[1040,256]{1,0:T(8,128)(2,1)}, u32[]{:S(2)}, u32[]{:S(2)}) collective-permute-start(bf16[1040,256]{1,0:T(8,128)(2,1)} %collective-permute-done.2.refs_5_.refs_9_), channel_id=1, source_target_pairs={{0,96},{16,112},{32,0},{48,16},{64,32},{80,48},{96,64},{112,80},{1... | collective-permute-start | bytes 1597448 | tf_op jit(solution)/shard_map/ppermute | solution.py:391
  32.1 4.5 %collective-permute-done.5.refs_3_.refs_7_ = bf16[1040,256]{1,0:T(8,128)(2,1)} collective-permute-done((bf16[1040,256]{1,0:T(8,128)(2,1)}, bf16[1040,256]{1,0:T(8,128)(2,1)}, u32[]{:S(2)}, u32[]{:S(2)}) %collective-permute-start.5) | collective-permute-done | bytes 532512 | tf_op jit(solution)/shard_map/ppermute | solution.py:391
  36.5 0.0 collective-permute-done.6.refs_4_.refs_8_
  36.5 13.0 %attend_near.1.refs_5_ = f32[2,1024,256]{2,1,0:T(8,128)} custom-call(s32[1]{0:T(128)S(6)} %copy.6.doc_ref, bf16[1040,256]{1,0:T(8,128)(2,1)} %get-tuple-element.16.refs_0_, bf16[1040,256]{1,0:T(8,128)(2,1)} %collective-permute-done.after_ref.refs_1_, bf16[1040,256]{1,0:T(8,128)(2,1)} %collective-permute-done.1.refs_2_.refs_6_, ...), custom_call_target="tpu_custom_call" | custom-call | flops 8589934592 | bytes 4194304 | tf_op jit(solution)/shard_map/attend_near/pallas_call | solution.py:340
  49.5 0.0 collective-permute-done.3.refs_2_
  49.5 0.0 collective-permute-done.4.refs_3_
  49.5 100.2 %attend_far.1 = bf16[4,2,256,128]{3,2,1,0:T(8,128)(2,1)} custom-call(s32[1]{0:T(128)S(6)} %copy.6.doc_ref, bf16[1040,256]{1,0:T(8,128)(2,1)} %get-tuple-element.16.refs_0_, bf16[1040,256]{1,0:T(8,128)(2,1)} %collective-permute-done.after_ref.refs_1_, bf16[1040,256]{1,0:T(8,128)(2,1)} %collective-permute-done.3.refs_2_, ...), custom_call_target="tpu_custom_call" | custom-call | flops 4294967296 | bytes 4194304 | tf_op jit(solution)/shard_map/attend_far/pallas_call | solution.py:340
  149.8 0.0 all-to-all-done.w_ref
  149.8 2.0 %collective-permute-start.8 = (bf16[4,128,2048]{2,1,0:T(8,128)(2,1)}, bf16[4,128,2048]{2,1,0:T(8,128)(2,1)S(1)}, u32[]{:S(2)}, u32[]{:S(2)}) collective-permute-start(bf16[4,128,2048]{2,1,0:T(8,128)(2,1)} %all-to-all-done.w_ref), channel_id=1, source_target_pairs={{0,16},{16,0},{32,48},{48,32},{64,80},{80,64},{96,112},{112,96},{1... | collective-permute-start | bytes 6291464 | tf_op jit(solution)/shard_map/ppermute | solution.py:391
  151.8 14.0 %all_to_all.15.ctx_ref = bf16[4,2,256,128]{3,2,1,0:T(8,128)(2,1)S(1)} all-to-all(bf16[4,2,256,128]{3,2,1,0:T(8,128)(2,1)} %attend_far.1), channel_id=1, replica_groups={{0,2,4,6},{8,10,12,14},{1,3,5,7},{9,11,13,15},{16,18,20,22},{24,26,28,3..., dimensions={0} | all-to-all | bytes 1048576 | tf_op jit(solution)/shard_map/all_to_all | solution.py:431
  165.8 0.0 collective-permute-start.7
  165.8 1.9 collective-permute-done.7.got_ref
  167.7 0.0 collective-permute-done.8.w_got_ref
  167.7 2.8 %output.1 = bf16[8,256,256]{2,1,0:T(8,128)(2,1)S(1)} custom-call(bf16[4,2,256,128]{3,2,1,0:T(8,128)(2,1)S(1)} %all_to_all.15.ctx_ref, bf16[4,2,256,128]{3,2,1,0:T(8,128)(2,1)S(1)} %collective-permute-done.7.got_ref, bf16[4,128,2048]{2,1,0:T(8,128)(2,1)} %all-to-all-done.w_ref, bf16[4,128,2048]{2,1,0:T(8,128)(2,1)S(1)} %collective-permute-done.8.w_got_ref), custom_call_target="tpu_custom_call" | custom-call | flops 1073741824 | bytes 6291456 | tf_op jit(solution)/shard_map/output/pallas_call | solution.py:376
  170.5 22.2 %all_to_all.16 = bf16[8,256,256]{2,1,0:T(8,128)(2,1)S(1)} all-to-all(bf16[8,256,256]{2,1,0:T(8,128)(2,1)S(1)} %output.1), channel_id=1, replica_groups=mesh['seq'=8,'head'=8,'batch'=2] {'head'}, dimensions={0} | all-to-all | bytes 2097152 | tf_op jit(solution)/shard_map/all_to_all | solution.py:433
  192.7 0.2 convert_element_type.6
  192.9 0.9 fusion
Async XLA Ops:
  6.1 8.2 %collective-permute-start = (bf16[1040,256]{1,0:T(8,128)(2,1)}, bf16[1040,256]{1,0:T(8,128)(2,1)}, u32[]{:S(2)}, u32[]{:S(2)}) collective-permute-start(bf16[1040,256]{1,0:T(8,128)(2,1)} %get-tuple-element.14), channel_id=1, source_target_pairs={{0,16},{16,0},{32,48},{48,32},{64,80},{80,64},{96,112},{112,96},{1... | collective-permute-start | bytes 1597448 | tf_op jit(solution)/shard_map/ppermute | solution.py:391
  6.2 22.6 %collective-permute-start.2 = (bf16[1040,256]{1,0:T(8,128)(2,1)}, bf16[1040,256]{1,0:T(8,128)(2,1)}, u32[]{:S(2)}, u32[]{:S(2)}) collective-permute-start(bf16[1040,256]{1,0:T(8,128)(2,1)} %get-tuple-element.14), channel_id=1, source_target_pairs={{0,112},{16,96},{32,16},{48,0},{64,48},{80,32},{96,80},{112,64},{1... | collective-permute-start | bytes 1597448 | tf_op jit(solution)/shard_map/ppermute | solution.py:391
  10.4 18.3 %collective-permute-start.1 = (bf16[1040,256]{1,0:T(8,128)(2,1)}, bf16[1040,256]{1,0:T(8,128)(2,1)}, u32[]{:S(2)}, u32[]{:S(2)}) collective-permute-start(bf16[1040,256]{1,0:T(8,128)(2,1)} %get-tuple-element.16.refs_0_), channel_id=1, source_target_pairs={{0,32},{16,48},{32,64},{48,80},{64,96},{80,112},{96,0},{112,16},{1... | collective-permute-start | bytes 1597448 | tf_op jit(solution)/shard_map/ppermute | solution.py:391
  10.4 26.1 %collective-permute-start.5 = (bf16[1040,256]{1,0:T(8,128)(2,1)}, bf16[1040,256]{1,0:T(8,128)(2,1)}, u32[]{:S(2)}, u32[]{:S(2)}) collective-permute-start(bf16[1040,256]{1,0:T(8,128)(2,1)} %get-tuple-element.14), channel_id=1, source_target_pairs={{0,48},{16,32},{32,80},{48,64},{64,112},{80,96},{96,16},{112,0},{1... | collective-permute-start | bytes 1597448 | tf_op jit(solution)/shard_map/ppermute | solution.py:391
  10.4 26.1 %collective-permute-start.6 = (bf16[1040,256]{1,0:T(8,128)(2,1)}, bf16[1040,256]{1,0:T(8,128)(2,1)}, u32[]{:S(2)}, u32[]{:S(2)}) collective-permute-start(bf16[1040,256]{1,0:T(8,128)(2,1)} %get-tuple-element.16.refs_0_), channel_id=1, source_target_pairs={{0,96},{16,112},{32,0},{48,16},{64,32},{80,48},{96,64},{112,80},{1... | collective-permute-start | bytes 1597448 | tf_op jit(solution)/shard_map/ppermute | solution.py:391
  16.7 133.1 %all-to-all-start = ((bf16[4,128,2048]{2,1,0:T(8,128)(2,1)}), bf16[4,128,2048]{2,1,0:T(8,128)(2,1)}, u32[]{:S(2)}, u32[]{:S(2)}) async-start(bf16[4,128,2048]{2,1,0:T(8,128)(2,1)} %spread.1), calls=%async_computation | async-start | bytes 4194304 | tf_op jit(solution)/shard_map/all_to_all | solution.py:405
  28.7 20.8 %collective-permute-start.3 = (bf16[1040,256]{1,0:T(8,128)(2,1)}, bf16[1040,256]{1,0:T(8,128)(2,1)}, u32[]{:S(2)}, u32[]{:S(2)}) collective-permute-start(bf16[1040,256]{1,0:T(8,128)(2,1)} %collective-permute-done.1.refs_2_.refs_6_), channel_id=1, source_target_pairs={{0,32},{16,48},{32,64},{48,80},{64,96},{80,112},{96,0},{112,16},{1... | collective-permute-start | bytes 1597448 | tf_op jit(solution)/shard_map/ppermute | solution.py:391
  28.8 20.7 %collective-permute-start.4 = (bf16[1040,256]{1,0:T(8,128)(2,1)}, bf16[1040,256]{1,0:T(8,128)(2,1)}, u32[]{:S(2)}, u32[]{:S(2)}) collective-permute-start(bf16[1040,256]{1,0:T(8,128)(2,1)} %collective-permute-done.2.refs_5_.refs_9_), channel_id=1, source_target_pairs={{0,96},{16,112},{32,0},{48,16},{64,32},{80,48},{96,64},{112,80},{1... | collective-permute-start | bytes 1597448 | tf_op jit(solution)/shard_map/ppermute | solution.py:391
  149.8 17.9 %collective-permute-start.8 = (bf16[4,128,2048]{2,1,0:T(8,128)(2,1)}, bf16[4,128,2048]{2,1,0:T(8,128)(2,1)S(1)}, u32[]{:S(2)}, u32[]{:S(2)}) collective-permute-start(bf16[4,128,2048]{2,1,0:T(8,128)(2,1)} %all-to-all-done.w_ref), channel_id=1, source_target_pairs={{0,16},{16,0},{32,48},{48,32},{64,80},{80,64},{96,112},{112,96},{1... | collective-permute-start | bytes 6291464 | tf_op jit(solution)/shard_map/ppermute | solution.py:391
  165.8 1.9 collective-permute-start.7

commit v2 on v1

--- a/solution.py
+++ b/solution.py
@@ -159,7 +159,7 @@
     else:
         q_refs, kv_refs, refs = refs[:2], refs[2 : 2 + count], refs[2 + count :]
         if last:
-            states, rest, refs = refs[:2], refs[2:6], refs[6:]
+            states, rest, refs = refs[:3], refs[3:7], refs[7:]
             out_ref, kv_scr, acc, sem, acc_sem, q_scr, sums, sums_sem, peak, weight_sum = refs
         else:
             out_ref, kv_scr, acc, sem, acc_sem, q_scr = refs
@@ -176,7 +176,7 @@
     )
     if last:
         added = start_all(
-            [pltpu.make_async_copy(states[i], sums.at[i], sums_sem.at[i]) for i in range(2)]
+            [pltpu.make_async_copy(states[i], sums.at[i], sums_sem.at[i]) for i in range(3)]
         )
     acc[...] = jnp.zeros_like(acc)
     for copy in copies:
@@ -304,7 +304,7 @@
 
     core = own_core()
     for q in range(2):
-        total = acc[q] + (sums[0, q] + sums[1, q])
+        total = (acc[q] + sums[0, q]) + (sums[1, q] + sums[2, q])
         inside = lax.broadcasted_iota(jnp.int32, (rows, HEAD_DIM), 0) + q_starts[q] < doc_len
         mixed = jnp.where(inside, total[:, :HEAD_DIM] / total[:, HEAD_DIM:], 0.0)
         block = core if q == 0 else 1 - core
@@ -329,8 +329,8 @@
     if last:
         args += [*states, *rest]
         scratch += [
-            pltpu.VMEM((2, *out_shape.shape), F32),
-            pltpu.SemaphoreType.DMA((2,)),
+            pltpu.VMEM((3, *out_shape.shape), F32),
+            pltpu.SemaphoreType.DMA((3,)),
         ]
         out_shape = jax.ShapeDtypeStruct((4, 2, rows // 4, HEAD_DIM), BF16)
         scratch += [
@@ -407,22 +407,32 @@
     )
     own_left, peer_right, here = lax.optimization_barrier((own_left, peer_right, here))
     own_far, peer_far = move(own_left, 1, 0), move(peer_right, -1, 0)
-    blocks = (own_left, peer_left, own_right, peer_right)
     near = attend(
         doc_length,
         queries,
-        blocks,
-        ((3, False), (3, True), (1, False), (1, True)),
+        (own_left, peer_right),
+        ((3, False), (1, True)),
         None,
         None,
         "attend_near",
     )
+    peer_left, own_right, near = lax.optimization_barrier((peer_left, own_right, near))
+    next_near = attend(
+        doc_length,
+        queries,
+        (peer_left, own_right),
+        ((3, True), (1, False)),
+        None,
+        None,
+        "attend_next",
+    )
+    blocks = (own_left, peer_left, own_right, peer_right)
     context = attend(
         doc_length,
         queries,
         (own_far, peer_far),
         ((2, False), (2, True)),
-        (here, near),
+        (here, near, next_near),
         blocks,
         "attend_far",
     )

time: 192 us -> 193 us (level); the launches traced: 194 us -> 193 us
    pallas_call x3 -> x4, Pallas kernels: 121 us -> 119 us  [attend(): pl.pallas_call(functools.partial(attend_kernel, places, first, last), in_...]
  transfers between devices with their start and end apart: 10 -> 10, of which waited for: 2 -> 2; matrix products, arithmetic and copies ran while one was open for 0% -> 0% of each run, Pallas kernels for 64% -> 63%
where the time goes in v2:
time: 193 us
  Pallas kernels  131 us (68%)
  blocking collectives  36.7 us (19%)
  starting transfers between devices  15.4 us (8%)
  waiting for transfers between devices  7.86 us (4%)
    pallas_call x4, Pallas kernels, attend(): pl.pallas_call(functools.partial(attend_kernel, places, first, last), in_...  119 us
    all_to_all x1, blocking collectives, body(): terms = lax.all_to_all(terms, 'head', 0, 0, tiled=True).astype(F32)  22.1 us
    all_to_all x1, blocking collectives, body(): lax.all_to_all(context, 'head', 0, 0, axis_index_groups=y_groups, tiled=T...  14.6 us
    ppermute x9, starting transfers between devices, move(): lax.ppermute(array, 'seq', [(i, (i // 2 + by) % 4 * 2 + (i % 2 ^ cross))...  10.9 us
    ppermute x9, waiting for transfers between devices, move(): lax.ppermute(array, 'seq', [(i, (i // 2 + by) % 4 * 2 + (i % 2 ^ cross))...  7.86 us
    pallas_call x1, Pallas kernels, project(): pl.pallas_call(project_kernel, in_specs=[ANY] * 3, out_specs=(ANY, ANY),...  6.07 us
    all_to_all x1, starting transfers between devices, body(): lax.all_to_all(repeated, 'head', 0, 0, axis_index_groups=y_groups, tiled=...  4.48 us
  transfers between devices with their start and end apart: 10, of which 2 were waited for; matrix products, arithmetic and copies ran while one was open for 0% of the time, Pallas kernels for 63%

profile of v2, /device:TPU:0, one launch (start us, length us, event | category | flops | bytes accessed | tf_op | source)
XLA Modules:
  0.0 192.6 jit_solution(7787690462862841478)
XLA Ops:
  0.0 6.1 %project.1 = (bf16[1040,256]{1,0:T(8,128)(2,1)}, bf16[1040,256]{1,0:T(8,128)(2,1)}) custom-call(bf16[1024,2048]{1,0:T(8,128)(2,1)} %x_ref.1, bf16[2048,256]{1,0:T(8,128)(2,1)} %ws_ref.1, bf16[2048,256]{1,0:T(8,128)(2,1)} %wv_ref.1), custom_call_target="tpu_custom_call" | custom-call | flops 2147483648 | bytes 7340032 | tf_op jit(solution)/shard_map/project/pallas_call | solution.py:110
  6.1 0.1 collective-permute-start
  6.2 4.2 %collective-permute-start.2 = (bf16[1040,256]{1,0:T(8,128)(2,1)}, bf16[1040,256]{1,0:T(8,128)(2,1)}, u32[]{:S(2)}, u32[]{:S(2)}) collective-permute-start(bf16[1040,256]{1,0:T(8,128)(2,1)} %get-tuple-element.17), channel_id=1, source_target_pairs={{0,112},{16,96},{32,16},{48,0},{64,48},{80,32},{96,80},{112,64},{1... | collective-permute-start | bytes 1597448 | tf_op jit(solution)/shard_map/ppermute | solution.py:391
  10.4 0.0 collective-permute-start.1
  10.4 0.0 collective-permute-start.5
  10.4 3.2 %collective-permute-start.6 = (bf16[1040,256]{1,0:T(8,128)(2,1)}, bf16[1040,256]{1,0:T(8,128)(2,1)}, u32[]{:S(2)}, u32[]{:S(2)}) collective-permute-start(bf16[1040,256]{1,0:T(8,128)(2,1)} %get-tuple-element.19.refs_0_), channel_id=1, source_target_pairs={{0,96},{16,112},{32,0},{48,16},{64,32},{80,48},{96,64},{112,80},{1... | collective-permute-start | bytes 1597448 | tf_op jit(solution)/shard_map/ppermute | solution.py:391
  14.3 0.0 collective-permute-done.after_ref.refs_1_
  14.3 2.4 %spread.1 = bf16[4,128,2048]{2,1,0:T(8,128)(2,1)} custom-call(bf16[256,2048]{1,0:T(8,128)(2,1)} %w_ref.1, bf16[1040,256]{1,0:T(8,128)(2,1)} %collective-permute-done.after_ref.refs_1_), custom_call_target="tpu_custom_call" | custom-call | tf_op jit(solution)/shard_map/spread/pallas_call | solution.py:142
  16.7 4.5 %all-to-all-start = ((bf16[4,128,2048]{2,1,0:T(8,128)(2,1)}), bf16[4,128,2048]{2,1,0:T(8,128)(2,1)}, u32[]{:S(2)}, u32[]{:S(2)}) async-start(bf16[4,128,2048]{2,1,0:T(8,128)(2,1)} %spread.1), calls=%async_computation | async-start | bytes 4194304 | tf_op jit(solution)/shard_map/all_to_all | solution.py:405
  21.2 7.5 %attend_here.1.refs_4_ = f32[2,1024,256]{2,1,0:T(8,128)} custom-call(s32[1]{0:T(128)S(6)} %copy.6.doc_ref, bf16[1040,256]{1,0:T(8,128)(2,1)} %get-tuple-element.19.refs_0_, bf16[1040,256]{1,0:T(8,128)(2,1)} %collective-permute-done.after_ref.refs_1_), custom_call_target="tpu_custom_call" | custom-call | flops 4294967296 | bytes 4194304 | tf_op jit(solution)/shard_map/attend_here/pallas_call | solution.py:340
  28.7 0.0 collective-permute-done.2.refs_3_.refs_10_
  28.7 0.0 collective-permute-done.1.refs_2_.refs_7_
  28.7 0.1 collective-permute-start.3
  28.8 3.2 %collective-permute-start.4 = (bf16[1040,256]{1,0:T(8,128)(2,1)}, bf16[1040,256]{1,0:T(8,128)(2,1)}, u32[]{:S(2)}, u32[]{:S(2)}) collective-permute-start(bf16[1040,256]{1,0:T(8,128)(2,1)} %collective-permute-done.2.refs_3_.refs_10_), channel_id=1, source_target_pairs={{0,96},{16,112},{32,0},{48,16},{64,32},{80,48},{96,64},{112,80},{1... | collective-permute-start | bytes 1597448 | tf_op jit(solution)/shard_map/ppermute | solution.py:391
  32.0 5.4 %attend_near.1.refs_5_ = f32[2,1024,256]{2,1,0:T(8,128)} custom-call(s32[1]{0:T(128)S(6)} %copy.6.doc_ref, bf16[1040,256]{1,0:T(8,128)(2,1)} %get-tuple-element.19.refs_0_, bf16[1040,256]{1,0:T(8,128)(2,1)} %collective-permute-done.after_ref.refs_1_, bf16[1040,256]{1,0:T(8,128)(2,1)} %collective-permute-done.1.refs_2_.refs_7_, ...), custom_call_target="tpu_custom_call" | custom-call | flops 4294967296 | bytes 4194304 | tf_op jit(solution)/shard_map/attend_near/pallas_call | solution.py:340
  37.4 0.0 collective-permute-done.5.refs_2_.refs_8_
  37.5 0.0 collective-permute-done.6.refs_3_.refs_9_
  37.5 5.4 %attend_next.1.refs_6_ = f32[2,1024,256]{2,1,0:T(8,128)} custom-call(s32[1]{0:T(128)S(6)} %copy.6.doc_ref, bf16[1040,256]{1,0:T(8,128)(2,1)} %get-tuple-element.19.refs_0_, bf16[1040,256]{1,0:T(8,128)(2,1)} %collective-permute-done.after_ref.refs_1_, bf16[1040,256]{1,0:T(8,128)(2,1)} %collective-permute-done.5.refs_2_.refs_8_, ...), custom_call_target="tpu_custom_call" | custom-call | flops 4294967296 | bytes 4194304 | tf_op jit(solution)/shard_map/attend_next/pallas_call | solution.py:340
  42.9 5.9 %collective-permute-done.3.refs_2_ = bf16[1040,256]{1,0:T(8,128)(2,1)} collective-permute-done((bf16[1040,256]{1,0:T(8,128)(2,1)}, bf16[1040,256]{1,0:T(8,128)(2,1)}, u32[]{:S(2)}, u32[]{:S(2)}) %collective-permute-start.3) | collective-permute-done | bytes 532512 | tf_op jit(solution)/shard_map/ppermute | solution.py:391
  48.8 0.0 collective-permute-done.4.refs_3_
  48.8 101.1 %attend_far.1 = bf16[4,2,256,128]{3,2,1,0:T(8,128)(2,1)} custom-call(s32[1]{0:T(128)S(6)} %copy.6.doc_ref, bf16[1040,256]{1,0:T(8,128)(2,1)} %get-tuple-element.19.refs_0_, bf16[1040,256]{1,0:T(8,128)(2,1)} %collective-permute-done.after_ref.refs_1_, bf16[1040,256]{1,0:T(8,128)(2,1)} %collective-permute-done.3.refs_2_, ...), custom_call_target="tpu_custom_call" | custom-call | flops 4294967296 | bytes 4194304 | tf_op jit(solution)/shard_map/attend_far/pallas_call | solution.py:340
  149.9 0.0 all-to-all-done.w_ref
  149.9 0.1 collective-permute-start.8
  150.0 14.6 %all_to_all.15.ctx_ref = bf16[4,2,256,128]{3,2,1,0:T(8,128)(2,1)S(1)} all-to-all(bf16[4,2,256,128]{3,2,1,0:T(8,128)(2,1)} %attend_far.1), channel_id=1, replica_groups={{0,2,4,6},{8,10,12,14},{1,3,5,7},{9,11,13,15},{16,18,20,22},{24,26,28,3..., dimensions={0} | all-to-all | bytes 1048576 | tf_op jit(solution)/shard_map/all_to_all | solution.py:441
  164.6 0.0 collective-permute-start.7
  164.6 1.9 collective-permute-done.7.got_ref
  166.5 0.0 collective-permute-done.8.w_got_ref
  166.5 2.8 %output.1 = bf16[8,256,256]{2,1,0:T(8,128)(2,1)S(1)} custom-call(bf16[4,2,256,128]{3,2,1,0:T(8,128)(2,1)S(1)} %all_to_all.15.ctx_ref, bf16[4,2,256,128]{3,2,1,0:T(8,128)(2,1)S(1)} %collective-permute-done.7.got_ref, bf16[4,128,2048]{2,1,0:T(8,128)(2,1)} %all-to-all-done.w_ref, bf16[4,128,2048]{2,1,0:T(8,128)(2,1)S(1)} %collective-permute-done.8.w_got_ref), custom_call_target="tpu_custom_call" | custom-call | flops 1073741824 | bytes 6291456 | tf_op jit(solution)/shard_map/output/pallas_call | solution.py:376
  169.4 22.1 %all_to_all.16 = bf16[8,256,256]{2,1,0:T(8,128)(2,1)S(1)} all-to-all(bf16[8,256,256]{2,1,0:T(8,128)(2,1)S(1)} %output.1), channel_id=1, replica_groups=mesh['seq'=8,'head'=8,'batch'=2] {'head'}, dimensions={0} | all-to-all | bytes 2097152 | tf_op jit(solution)/shard_map/all_to_all | solution.py:443
  191.5 0.2 convert_element_type.6
  191.7 0.9 fusion
Async XLA Ops:
  6.1 8.2 %collective-permute-start = (bf16[1040,256]{1,0:T(8,128)(2,1)}, bf16[1040,256]{1,0:T(8,128)(2,1)}, u32[]{:S(2)}, u32[]{:S(2)}) collective-permute-start(bf16[1040,256]{1,0:T(8,128)(2,1)} %get-tuple-element.17), channel_id=1, source_target_pairs={{0,16},{16,0},{32,48},{48,32},{64,80},{80,64},{96,112},{112,96},{1... | collective-permute-start | bytes 1597448 | tf_op jit(solution)/shard_map/ppermute | solution.py:391
  6.2 22.6 %collective-permute-start.2 = (bf16[1040,256]{1,0:T(8,128)(2,1)}, bf16[1040,256]{1,0:T(8,128)(2,1)}, u32[]{:S(2)}, u32[]{:S(2)}) collective-permute-start(bf16[1040,256]{1,0:T(8,128)(2,1)} %get-tuple-element.17), channel_id=1, source_target_pairs={{0,112},{16,96},{32,16},{48,0},{64,48},{80,32},{96,80},{112,64},{1... | collective-permute-start | bytes 1597448 | tf_op jit(solution)/shard_map/ppermute | solution.py:391
  10.4 18.3 %collective-permute-start.1 = (bf16[1040,256]{1,0:T(8,128)(2,1)}, bf16[1040,256]{1,0:T(8,128)(2,1)}, u32[]{:S(2)}, u32[]{:S(2)}) collective-permute-start(bf16[1040,256]{1,0:T(8,128)(2,1)} %get-tuple-element.19.refs_0_), channel_id=1, source_target_pairs={{0,32},{16,48},{32,64},{48,80},{64,96},{80,112},{96,0},{112,16},{1... | collective-permute-start | bytes 1597448 | tf_op jit(solution)/shard_map/ppermute | solution.py:391
  10.4 27.0 %collective-permute-start.5 = (bf16[1040,256]{1,0:T(8,128)(2,1)}, bf16[1040,256]{1,0:T(8,128)(2,1)}, u32[]{:S(2)}, u32[]{:S(2)}) collective-permute-start(bf16[1040,256]{1,0:T(8,128)(2,1)} %get-tuple-element.17), channel_id=1, source_target_pairs={{0,48},{16,32},{32,80},{48,64},{64,112},{80,96},{96,16},{112,0},{1... | collective-permute-start | bytes 1597448 | tf_op jit(solution)/shard_map/ppermute | solution.py:391
  10.4 27.0 %collective-permute-start.6 = (bf16[1040,256]{1,0:T(8,128)(2,1)}, bf16[1040,256]{1,0:T(8,128)(2,1)}, u32[]{:S(2)}, u32[]{:S(2)}) collective-permute-start(bf16[1040,256]{1,0:T(8,128)(2,1)} %get-tuple-element.19.refs_0_), channel_id=1, source_target_pairs={{0,96},{16,112},{32,0},{48,16},{64,32},{80,48},{96,64},{112,80},{1... | collective-permute-start | bytes 1597448 | tf_op jit(solution)/shard_map/ppermute | solution.py:391
  16.7 133.2 %all-to-all-start = ((bf16[4,128,2048]{2,1,0:T(8,128)(2,1)}), bf16[4,128,2048]{2,1,0:T(8,128)(2,1)}, u32[]{:S(2)}, u32[]{:S(2)}) async-start(bf16[4,128,2048]{2,1,0:T(8,128)(2,1)} %spread.1), calls=%async_computation | async-start | bytes 4194304 | tf_op jit(solution)/shard_map/all_to_all | solution.py:405
  28.7 20.1 %collective-permute-start.3 = (bf16[1040,256]{1,0:T(8,128)(2,1)}, bf16[1040,256]{1,0:T(8,128)(2,1)}, u32[]{:S(2)}, u32[]{:S(2)}) collective-permute-start(bf16[1040,256]{1,0:T(8,128)(2,1)} %collective-permute-done.1.refs_2_.refs_7_), channel_id=1, source_target_pairs={{0,32},{16,48},{32,64},{48,80},{64,96},{80,112},{96,0},{112,16},{1... | collective-permute-start | bytes 1597448 | tf_op jit(solution)/shard_map/ppermute | solution.py:391
  28.8 20.0 %collective-permute-start.4 = (bf16[1040,256]{1,0:T(8,128)(2,1)}, bf16[1040,256]{1,0:T(8,128)(2,1)}, u32[]{:S(2)}, u32[]{:S(2)}) collective-permute-start(bf16[1040,256]{1,0:T(8,128)(2,1)} %collective-permute-done.2.refs_3_.refs_10_), channel_id=1, source_target_pairs={{0,96},{16,112},{32,0},{48,16},{64,32},{80,48},{96,64},{112,80},{1... | collective-permute-start | bytes 1597448 | tf_op jit(solution)/shard_map/ppermute | solution.py:391
  149.9 16.6 %collective-permute-start.8 = (bf16[4,128,2048]{2,1,0:T(8,128)(2,1)}, bf16[4,128,2048]{2,1,0:T(8,128)(2,1)S(1)}, u32[]{:S(2)}, u32[]{:S(2)}) collective-permute-start(bf16[4,128,2048]{2,1,0:T(8,128)(2,1)} %all-to-all-done.w_ref), channel_id=1, source_target_pairs={{0,16},{16,0},{32,48},{48,32},{64,80},{80,64},{96,112},{112,96},{1... | collective-permute-start | bytes 6291464 | tf_op jit(solution)/shard_map/ppermute | solution.py:391
  164.6 1.9 collective-permute-start.7

commit v3 on v1

--- a/solution.py
+++ b/solution.py
@@ -430,8 +430,8 @@
     weights_got = move(weights, 0, 1)
     context = lax.all_to_all(context, "head", 0, 0, axis_index_groups=y_groups, tiled=True)
     terms = output(context, move(context, 0, 1), weights, weights_got)
-    terms = lax.all_to_all(terms, "head", 0, 0, tiled=True).astype(F32)
-    result = (terms[:4] + terms[4:]).astype(BF16)
+    terms = lax.all_to_all(terms, "head", 0, 0, tiled=True)
+    result = (terms[:4].astype(F32) + terms[4:].astype(F32)).astype(BF16)
     return result.reshape(tokens.shape[0], result.shape[-1])
 
 

time: 192 us -> 191 us (level)
  Pallas kernels: 132 us -> 127 us
  waiting for transfers between devices: 6.41 us -> 10.6 us
    pallas_call x3, Pallas kernels: 121 us -> 116 us  [attend(): pl.pallas_call(functools.partial(attend_kernel, places, first, last), in_...]
    ppermute x9, waiting for transfers between devices: 6.4 us -> 10.6 us  [move(): lax.ppermute(array, 'seq', [(i, (i // 2 + by) % 4 * 2 + (i % 2 ^ cross))...]
  transfers between devices with their start and end apart: 10 -> 10, of which waited for: 2 -> 3; matrix products, arithmetic and copies ran while one was open for 0% -> 0% of each run, Pallas kernels for 64% -> 62%
where the time goes in v3:
time: 191 us; the launch traced here: 192 us
  Pallas kernels  127 us (66%)
  blocking collectives  36.8 us (19%)
  starting transfers between devices  15.4 us (8%)
  waiting for transfers between devices  10.6 us (6%)
    pallas_call x3, Pallas kernels, attend(): pl.pallas_call(functools.partial(attend_kernel, places, first, last), in_...  116 us
    all_to_all x1, blocking collectives, body(): terms = lax.all_to_all(terms, 'head', 0, 0, tiled=True)  22.2 us
    all_to_all x1, blocking collectives, body(): lax.all_to_all(context, 'head', 0, 0, axis_index_groups=y_groups, tiled=T...  14.6 us
    ppermute x9, starting transfers between devices, move(): lax.ppermute(array, 'seq', [(i, (i // 2 + by) % 4 * 2 + (i % 2 ^ cross))...  10.9 us
    ppermute x9, waiting for transfers between devices, move(): lax.ppermute(array, 'seq', [(i, (i // 2 + by) % 4 * 2 + (i % 2 ^ cross))...  10.6 us
    pallas_call x1, Pallas kernels, project(): pl.pallas_call(project_kernel, in_specs=[ANY] * 3, out_specs=(ANY, ANY),...  6.07 us
    all_to_all x1, starting transfers between devices, body(): lax.all_to_all(repeated, 'head', 0, 0, axis_index_groups=y_groups, tiled=...  4.48 us
  transfers between devices with their start and end apart: 10, of which 3 were waited for; matrix products, arithmetic and copies ran while one was open for 0% of the time, Pallas kernels for 62%

profile of v3, /device:TPU:0, one launch (start us, length us, event | category | flops | bytes accessed | tf_op | source)
XLA Modules:
  0.0 191.6 jit_solution(15778235113732609075)
XLA Ops:
  0.0 6.1 %project.1 = (bf16[1040,256]{1,0:T(8,128)(2,1)}, bf16[1040,256]{1,0:T(8,128)(2,1)}) custom-call(bf16[1024,2048]{1,0:T(8,128)(2,1)} %x_ref.1, bf16[2048,256]{1,0:T(8,128)(2,1)} %ws_ref.1, bf16[2048,256]{1,0:T(8,128)(2,1)} %wv_ref.1), custom_call_target="tpu_custom_call" | custom-call | flops 2147483648 | bytes 7340032 | tf_op jit(solution)/shard_map/project/pallas_call | solution.py:110
  6.1 0.1 collective-permute-start
  6.2 4.2 %collective-permute-start.2 = (bf16[1040,256]{1,0:T(8,128)(2,1)}, bf16[1040,256]{1,0:T(8,128)(2,1)}, u32[]{:S(2)}, u32[]{:S(2)}) collective-permute-start(bf16[1040,256]{1,0:T(8,128)(2,1)} %get-tuple-element.14), channel_id=1, source_target_pairs={{0,112},{16,96},{32,16},{48,0},{64,48},{80,32},{96,80},{112,64},{1... | collective-permute-start | bytes 1597448 | tf_op jit(solution)/shard_map/ppermute | solution.py:391
  10.4 0.0 collective-permute-start.1
  10.4 0.0 collective-permute-start.5
  10.4 3.2 %collective-permute-start.6 = (bf16[1040,256]{1,0:T(8,128)(2,1)}, bf16[1040,256]{1,0:T(8,128)(2,1)}, u32[]{:S(2)}, u32[]{:S(2)}) collective-permute-start(bf16[1040,256]{1,0:T(8,128)(2,1)} %get-tuple-element.16.refs_0_), channel_id=1, source_target_pairs={{0,96},{16,112},{32,0},{48,16},{64,32},{80,48},{96,64},{112,80},{1... | collective-permute-start | bytes 1597448 | tf_op jit(solution)/shard_map/ppermute | solution.py:391
  14.3 0.0 collective-permute-done.after_ref.refs_1_
  14.3 2.4 %spread.1 = bf16[4,128,2048]{2,1,0:T(8,128)(2,1)} custom-call(bf16[256,2048]{1,0:T(8,128)(2,1)} %w_ref.1, bf16[1040,256]{1,0:T(8,128)(2,1)} %collective-permute-done.after_ref.refs_1_), custom_call_target="tpu_custom_call" | custom-call | tf_op jit(solution)/shard_map/spread/pallas_call | solution.py:142
  16.7 4.5 %all-to-all-start = ((bf16[4,128,2048]{2,1,0:T(8,128)(2,1)}), bf16[4,128,2048]{2,1,0:T(8,128)(2,1)}, u32[]{:S(2)}, u32[]{:S(2)}) async-start(bf16[4,128,2048]{2,1,0:T(8,128)(2,1)} %spread.1), calls=%async_computation | async-start | bytes 4194304 | tf_op jit(solution)/shard_map/all_to_all | solution.py:405
  21.2 7.5 %attend_here.1.refs_4_ = f32[2,1024,256]{2,1,0:T(8,128)} custom-call(s32[1]{0:T(128)S(6)} %copy.6.doc_ref, bf16[1040,256]{1,0:T(8,128)(2,1)} %get-tuple-element.16.refs_0_, bf16[1040,256]{1,0:T(8,128)(2,1)} %collective-permute-done.after_ref.refs_1_), custom_call_target="tpu_custom_call" | custom-call | flops 4294967296 | bytes 4194304 | tf_op jit(solution)/shard_map/attend_here/pallas_call | solution.py:340
  28.7 0.0 collective-permute-done.2.refs_5_.refs_9_
  28.7 0.0 collective-permute-done.1.refs_2_.refs_6_
  28.7 0.1 collective-permute-start.3
  28.8 3.2 %collective-permute-start.4 = (bf16[1040,256]{1,0:T(8,128)(2,1)}, bf16[1040,256]{1,0:T(8,128)(2,1)}, u32[]{:S(2)}, u32[]{:S(2)}) collective-permute-start(bf16[1040,256]{1,0:T(8,128)(2,1)} %collective-permute-done.2.refs_5_.refs_9_), channel_id=1, source_target_pairs={{0,96},{16,112},{32,0},{48,16},{64,32},{80,48},{96,64},{112,80},{1... | collective-permute-start | bytes 1597448 | tf_op jit(solution)/shard_map/ppermute | solution.py:391
  32.1 4.5 %collective-permute-done.5.refs_3_.refs_7_ = bf16[1040,256]{1,0:T(8,128)(2,1)} collective-permute-done((bf16[1040,256]{1,0:T(8,128)(2,1)}, bf16[1040,256]{1,0:T(8,128)(2,1)}, u32[]{:S(2)}, u32[]{:S(2)}) %collective-permute-start.5) | collective-permute-done | bytes 532512 | tf_op jit(solution)/shard_map/ppermute | solution.py:391
  36.5 0.0 collective-permute-done.6.refs_4_.refs_8_
  36.5 8.0 %attend_near.1.refs_5_ = f32[2,1024,256]{2,1,0:T(8,128)} custom-call(s32[1]{0:T(128)S(6)} %copy.6.doc_ref, bf16[1040,256]{1,0:T(8,128)(2,1)} %get-tuple-element.16.refs_0_, bf16[1040,256]{1,0:T(8,128)(2,1)} %collective-permute-done.after_ref.refs_1_, bf16[1040,256]{1,0:T(8,128)(2,1)} %collective-permute-done.1.refs_2_.refs_6_, ...), custom_call_target="tpu_custom_call" | custom-call | flops 8589934592 | bytes 4194304 | tf_op jit(solution)/shard_map/attend_near/pallas_call | solution.py:340
  44.6 4.2 %collective-permute-done.3.refs_2_ = bf16[1040,256]{1,0:T(8,128)(2,1)} collective-permute-done((bf16[1040,256]{1,0:T(8,128)(2,1)}, bf16[1040,256]{1,0:T(8,128)(2,1)}, u32[]{:S(2)}, u32[]{:S(2)}) %collective-permute-start.3) | collective-permute-done | bytes 532512 | tf_op jit(solution)/shard_map/ppermute | solution.py:391
  48.8 0.0 collective-permute-done.4.refs_3_
  48.8 100.2 %attend_far.1 = bf16[4,2,256,128]{3,2,1,0:T(8,128)(2,1)} custom-call(s32[1]{0:T(128)S(6)} %copy.6.doc_ref, bf16[1040,256]{1,0:T(8,128)(2,1)} %get-tuple-element.16.refs_0_, bf16[1040,256]{1,0:T(8,128)(2,1)} %collective-permute-done.after_ref.refs_1_, bf16[1040,256]{1,0:T(8,128)(2,1)} %collective-permute-done.3.refs_2_, ...), custom_call_target="tpu_custom_call" | custom-call | flops 4294967296 | bytes 4194304 | tf_op jit(solution)/shard_map/attend_far/pallas_call | solution.py:340
  149.1 0.0 all-to-all-done.w_ref
  149.1 0.1 collective-permute-start.8
  149.2 14.6 %all_to_all.15.ctx_ref = bf16[4,2,256,128]{3,2,1,0:T(8,128)(2,1)S(1)} all-to-all(bf16[4,2,256,128]{3,2,1,0:T(8,128)(2,1)} %attend_far.1), channel_id=1, replica_groups={{0,2,4,6},{8,10,12,14},{1,3,5,7},{9,11,13,15},{16,18,20,22},{24,26,28,3..., dimensions={0} | all-to-all | bytes 1048576 | tf_op jit(solution)/shard_map/all_to_all | solution.py:431
  163.8 0.0 collective-permute-start.7
  163.8 1.9 collective-permute-done.7.got_ref
  165.7 0.0 collective-permute-done.8.w_got_ref
  165.7 2.8 %output.1 = bf16[8,256,256]{2,1,0:T(8,128)(2,1)S(1)} custom-call(bf16[4,2,256,128]{3,2,1,0:T(8,128)(2,1)S(1)} %all_to_all.15.ctx_ref, bf16[4,2,256,128]{3,2,1,0:T(8,128)(2,1)S(1)} %collective-permute-done.7.got_ref, bf16[4,128,2048]{2,1,0:T(8,128)(2,1)} %all-to-all-done.w_ref, bf16[4,128,2048]{2,1,0:T(8,128)(2,1)S(1)} %collective-permute-done.8.w_got_ref), custom_call_target="tpu_custom_call" | custom-call | flops 1073741824 | bytes 6291456 | tf_op jit(solution)/shard_map/output/pallas_call | solution.py:376
  168.6 22.2 %all_to_all.16 = bf16[8,256,256]{2,1,0:T(8,128)(2,1)S(1)} all-to-all(bf16[8,256,256]{2,1,0:T(8,128)(2,1)S(1)} %output.1), channel_id=1, replica_groups=mesh['seq'=8,'head'=8,'batch'=2] {'head'}, dimensions={0} | all-to-all | bytes 2097152 | tf_op jit(solution)/shard_map/all_to_all | solution.py:433
  190.7 0.9 add_convert_fusion
Async XLA Ops:
  6.1 8.2 %collective-permute-start = (bf16[1040,256]{1,0:T(8,128)(2,1)}, bf16[1040,256]{1,0:T(8,128)(2,1)}, u32[]{:S(2)}, u32[]{:S(2)}) collective-permute-start(bf16[1040,256]{1,0:T(8,128)(2,1)} %get-tuple-element.14), channel_id=1, source_target_pairs={{0,16},{16,0},{32,48},{48,32},{64,80},{80,64},{96,112},{112,96},{1... | collective-permute-start | bytes 1597448 | tf_op jit(solution)/shard_map/ppermute | solution.py:391
  6.2 22.6 %collective-permute-start.2 = (bf16[1040,256]{1,0:T(8,128)(2,1)}, bf16[1040,256]{1,0:T(8,128)(2,1)}, u32[]{:S(2)}, u32[]{:S(2)}) collective-permute-start(bf16[1040,256]{1,0:T(8,128)(2,1)} %get-tuple-element.14), channel_id=1, source_target_pairs={{0,112},{16,96},{32,16},{48,0},{64,48},{80,32},{96,80},{112,64},{1... | collective-permute-start | bytes 1597448 | tf_op jit(solution)/shard_map/ppermute | solution.py:391
  10.4 18.3 %collective-permute-start.1 = (bf16[1040,256]{1,0:T(8,128)(2,1)}, bf16[1040,256]{1,0:T(8,128)(2,1)}, u32[]{:S(2)}, u32[]{:S(2)}) collective-permute-start(bf16[1040,256]{1,0:T(8,128)(2,1)} %get-tuple-element.16.refs_0_), channel_id=1, source_target_pairs={{0,32},{16,48},{32,64},{48,80},{64,96},{80,112},{96,0},{112,16},{1... | collective-permute-start | bytes 1597448 | tf_op jit(solution)/shard_map/ppermute | solution.py:391
  10.4 26.1 %collective-permute-start.5 = (bf16[1040,256]{1,0:T(8,128)(2,1)}, bf16[1040,256]{1,0:T(8,128)(2,1)}, u32[]{:S(2)}, u32[]{:S(2)}) collective-permute-start(bf16[1040,256]{1,0:T(8,128)(2,1)} %get-tuple-element.14), channel_id=1, source_target_pairs={{0,48},{16,32},{32,80},{48,64},{64,112},{80,96},{96,16},{112,0},{1... | collective-permute-start | bytes 1597448 | tf_op jit(solution)/shard_map/ppermute | solution.py:391
  10.4 26.1 %collective-permute-start.6 = (bf16[1040,256]{1,0:T(8,128)(2,1)}, bf16[1040,256]{1,0:T(8,128)(2,1)}, u32[]{:S(2)}, u32[]{:S(2)}) collective-permute-start(bf16[1040,256]{1,0:T(8,128)(2,1)} %get-tuple-element.16.refs_0_), channel_id=1, source_target_pairs={{0,96},{16,112},{32,0},{48,16},{64,32},{80,48},{96,64},{112,80},{1... | collective-permute-start | bytes 1597448 | tf_op jit(solution)/shard_map/ppermute | solution.py:391
  16.7 132.4 %all-to-all-start = ((bf16[4,128,2048]{2,1,0:T(8,128)(2,1)}), bf16[4,128,2048]{2,1,0:T(8,128)(2,1)}, u32[]{:S(2)}, u32[]{:S(2)}) async-start(bf16[4,128,2048]{2,1,0:T(8,128)(2,1)} %spread.1), calls=%async_computation | async-start | bytes 4194304 | tf_op jit(solution)/shard_map/all_to_all | solution.py:405
  28.7 20.1 %collective-permute-start.3 = (bf16[1040,256]{1,0:T(8,128)(2,1)}, bf16[1040,256]{1,0:T(8,128)(2,1)}, u32[]{:S(2)}, u32[]{:S(2)}) collective-permute-start(bf16[1040,256]{1,0:T(8,128)(2,1)} %collective-permute-done.1.refs_2_.refs_6_), channel_id=1, source_target_pairs={{0,32},{16,48},{32,64},{48,80},{64,96},{80,112},{96,0},{112,16},{1... | collective-permute-start | bytes 1597448 | tf_op jit(solution)/shard_map/ppermute | solution.py:391
  28.8 20.0 %collective-permute-start.4 = (bf16[1040,256]{1,0:T(8,128)(2,1)}, bf16[1040,256]{1,0:T(8,128)(2,1)}, u32[]{:S(2)}, u32[]{:S(2)}) collective-permute-start(bf16[1040,256]{1,0:T(8,128)(2,1)} %collective-permute-done.2.refs_5_.refs_9_), channel_id=1, source_target_pairs={{0,96},{16,112},{32,0},{48,16},{64,32},{80,48},{96,64},{112,80},{1... | collective-permute-start | bytes 1597448 | tf_op jit(solution)/shard_map/ppermute | solution.py:391
  149.1 16.6 %collective-permute-start.8 = (bf16[4,128,2048]{2,1,0:T(8,128)(2,1)}, bf16[4,128,2048]{2,1,0:T(8,128)(2,1)S(1)}, u32[]{:S(2)}, u32[]{:S(2)}) collective-permute-start(bf16[4,128,2048]{2,1,0:T(8,128)(2,1)} %all-to-all-done.w_ref), channel_id=1, source_target_pairs={{0,16},{16,0},{32,48},{48,32},{64,80},{80,64},{96,112},{112,96},{1... | collective-permute-start | bytes 6291464 | tf_op jit(solution)/shard_map/ppermute | solution.py:391
  163.8 1.9 collective-permute-start.7
